TPU v7x, 512 devices: a whole 4x4x16 slice. The times are simulated.
512 devices in a mesh: dp: 64 (over x, z), tensor: 8 (over y, core).
Axes of the slice: x: 4, y: 4, z: 16, core: 2. Of those that a mesh axis runs over, the one named last changes fastest.
Arguments:
- inputs: bfloat16 [16384, 1024], P('dp'), may hold values from -6 to 6
- out_grad: bfloat16 [16384, 8192], P('dp', 'tensor')
- left_stat: float32 [64, 512, 512], P('dp', 'tensor')
- right_stat: float32 [64, 512, 512], P('dp', 'tensor')
- left_root: float32 [64, 512, 512], P('dp', 'tensor')
- right_root: float32 [64, 512, 512], P('dp', 'tensor'), as said below
- owner_blocks: int32 [64, 1], replicated, may hold values from 0 to 32, as said below
Outputs:
- left_new: float32 [64, 512, 512], P('dp', 'tensor')
- right_new: float32 [64, 512, 512], P('dp', 'tensor')
- direction: bfloat16 [1024, 8192], P('dp', 'tensor')
Inputs may be any that keep to these rules, and one draw needn't show every extreme that they name: `owner_blocks`: each of the 32 blocks appears in exactly one slot; every other slot holds 32; some owners hold a block while others hold none. `right_root`: each slot's matrix is symmetric.
All inputs are finite; a program needn't handle non-finite values.
Results may differ from a plain program's by a relative error of at most 0.00115.
Values may be sent and summed in bfloat16 or wider, within the bound.
A program may use at most 64 MiB of HBM per device.

v0:
```python
import jax
import jax.numpy as jnp
from jax import lax
from jax.sharding import PartitionSpec as P

BLK = 512
RB = 2
CBD = 2
CAP = 1
NBD = 4


FACTOR_DECAY = 0.9
GRAFT_EPSILON = 1e-06


def on_device(inputs, out_grad, left_stat, right_stat, left_root, right_root, owner_blocks):
    replica_count = lax.axis_size("dp")
    tensor_count = lax.axis_size("tensor")
    own_index = lax.axis_index("dp")
    column_group = lax.axis_index("tensor")
    token_count = inputs.shape[0]
    rows_per_replica = BLK // replica_count
    rows_tensor = BLK // tensor_count
    shard_rows = RB * BLK // replica_count
    row_pieces = BLK // shard_rows
    input_activations = inputs.reshape(token_count, RB, BLK)
    output_gradients = out_grad.reshape(token_count, CBD, BLK)
    gram_contribution = jnp.einsum(
        "osz,ofx->zsfx", input_activations, output_gradients, preferred_element_type=jnp.float32
    )
    reduced_sum = lax.psum_scatter(
        gram_contribution.reshape(lax.axis_size("dp") * rows_per_replica, NBD, BLK),
        "dp",
        scatter_dimension=0,
        tiled=True,
    )
    block_ids = column_group * NBD + jnp.arange(NBD, dtype=jnp.int32)
    selector = (owner_blocks[:, :, None] == block_ids[None, None, :]).astype(jnp.float32)
    outgoing = jnp.einsum("osj,rjc->sorc", selector, reduced_sum, precision=lax.Precision.HIGHEST)
    incoming = lax.all_to_all(outgoing, "dp", split_axis=1, concat_axis=1, tiled=True)
    owned = lax.psum(incoming.reshape(CAP, BLK, BLK), "tensor")
    first_local = column_group * rows_tensor
    grad_rows = lax.dynamic_slice_in_dim(owned, first_local, rows_tensor, 1)
    grad_cols = lax.dynamic_slice_in_dim(owned, first_local, rows_tensor, 2)
    fraction = (1.0 - FACTOR_DECAY) / BLK
    left_gram_matrix = jnp.einsum("sac,sbc->sab", grad_rows, owned, precision=lax.Precision.HIGHEST)
    right_gram = jnp.einsum("sac,sab->scb", grad_cols, owned, precision=lax.Precision.HIGHEST)
    left_new = FACTOR_DECAY * left_stat + fraction * left_gram_matrix
    right_new = FACTOR_DECAY * right_stat + fraction * right_gram
    turned = jnp.einsum("sck,sak->sca", right_root, owned, precision=lax.Precision.HIGHEST)
    precond = jnp.einsum(
        "sra,sca->src",
        left_root,
        lax.all_gather(turned, "tensor", axis=1, tiled=True),
        precision=lax.Precision.HIGHEST,
    )
    grad_square = jnp.mean(owned * owned, axis=(1, 2))
    local_square = jnp.sum(precond * precond, axis=(1, 2))
    prec_square = lax.psum(local_square, "tensor") / (BLK * BLK)
    graft_scale = jnp.sqrt((grad_square + GRAFT_EPSILON) / (prec_square + GRAFT_EPSILON))
    update_rows = (precond * graft_scale[:, None, None]).astype(jnp.bfloat16)
    updates = lax.all_gather(update_rows, "tensor", axis=1, tiled=True)
    slot_blocks = owner_blocks[own_index]
    block_group = slot_blocks // NBD
    block_rowblock = slot_blocks % NBD // CBD
    send_mask = (
        (block_group == column_group)[:, None]
        & (block_rowblock[:, None] == jnp.arange(RB, dtype=jnp.int32)[None, :])
    ).astype(jnp.bfloat16)
    stacked = updates.reshape(CAP, row_pieces, shard_rows, BLK)
    outgoing_back = stacked[:, None] * send_mask[:, :, None, None, None]
    outgoing_back = outgoing_back.reshape(CAP, RB * row_pieces, shard_rows, BLK)
    arrived = lax.all_to_all(outgoing_back, "dp", split_axis=1, concat_axis=1, tiled=True)
    my_rowblock = own_index // row_pieces
    wanted = column_group * NBD + my_rowblock * CBD + jnp.arange(CBD, dtype=jnp.int32)
    chooser = (owner_blocks[:, :, None] == wanted[None, None, :]).astype(jnp.bfloat16)
    direction = jnp.einsum("osb,sohc->hbc", chooser, arrived, preferred_element_type=jnp.float32)
    direction = direction.astype(jnp.bfloat16).reshape(shard_rows, CBD * BLK)
    return (left_new, right_new, direction)


def solution(mesh):
    placed = (
        P("dp", None),
        P("dp", "tensor"),
        P("dp", "tensor", None),
        P("dp", "tensor", None),
        P("dp", "tensor", None),
        P("dp", "tensor", None),
        P(),
    )
    return jax.shard_map(
        on_device,
        mesh=mesh,
        in_specs=placed,
        out_specs=(P("dp", "tensor", None), P("dp", "tensor", None), P("dp", "tensor")),
        check_vma=False,
    )
```

profile of v0, /device:TPU:1, one launch (start us, length us, event | category | flops | bytes accessed | tf_op | source)
XLA Modules:
  0.0 988.8 jit_solution(7137354609403608520)
XLA Ops:
  7.2 0.0 copy-start
  7.2 0.0 reduce-scatter.2.cloned.1.call-start
  7.2 1.3 copy.26
  8.5 3.7 convolution_bitcast_fusion
  12.2 5.2 copy.21
  17.5 0.0 copy-start.5
  17.5 0.0 reduce-scatter.2.cloned.1.call-update
  17.5 0.0 copy-start.2
  17.5 0.0 all-reduce.2.cloned.1.call-start
  17.6 694.2 %reduce-scatter.2.cloned.1.call-done = f32[8,4,512]{2,0,1:T(8,128)} async-done(((f32[512,4,512]{2,0,1:T(8,128)}), f32[8,4,512]{2,0,1:T(8,128)}) %reduce-scatter.2.cloned.1.call-update) | async-done | bytes 65552 | tf_op jit(solution)/shard_map/reduce_scatter | solution.py:32
  711.8 0.0 copy-done.5
  711.8 1.6 convolution_bitcast_fusion.1
  713.4 0.6 copy.23
  714.0 48.7 %all_to_all.10 = f32[1,64,8,512]{3,2,0,1:T(8,128)} all-to-all(f32[1,64,8,512]{3,2,0,1:T(8,128)S(1)} %copy.23), channel_id=1, replica_groups=mesh['dp'=64,'tensor'=8] {'dp'}, dimensions={1} | all-to-all | bytes 2097152 | tf_op jit(solution)/shard_map/all_to_all | solution.py:41
  762.7 0.0 all-reduce.2.cloned.1.call-update
  762.7 0.0 copy-start.3
  762.7 0.0 all-gather.4.cloned.1.call-start
  762.8 84.5 %all-reduce.2.cloned.1.call-done = f32[1,512,512]{2,1,0:T(8,128)} async-done(((f32[1,512,512]{2,1,0:T(8,128)}), f32[1,512,512]{2,1,0:T(8,128)}) %all-reduce.2.cloned.1.call-update) | async-done | bytes 1048592 | tf_op jit(solution)/shard_map/psum | solution.py:42
  847.3 0.0 copy-done.2
  847.3 0.0 copy-start.1
  847.3 3.1 convolution_bitcast_fusion.2
  850.4 0.0 copy-start.4
  850.4 0.0 all-gather.4.cloned.1.call-update
  850.4 0.6 constant_dynamic-slice_fusion
  853.6 0.1 mul.94
  853.7 0.1 mul.95
  853.8 2.1 multiply_reduce_fusion
  856.6 26.6 %all-gather.4.cloned.1.call-done = f32[512,512]{1,0:T(8,128)} async-done(((f32[64,512]{1,0:T(8,128)}), f32[512,512]{1,0:T(8,128)}) %all-gather.4.cloned.1.call-update) | async-done | bytes 1048592 | tf_op jit(solution)/shard_map/all_gather | solution.py:55
  883.2 0.0 copy-done
  883.2 3.0 multiply_reduce_fusion.1
  886.2 12.6 %psum.15 = f32[1]{0:T(128)} all-reduce(f32[1]{0:T(128)} %bitcast.20), channel_id=1, replica_groups=mesh['dp'=64,'tensor'=8] {'tensor'}, use_global_device_ids=true, to_apply=%region_4.0 | all-reduce | flops 1 | bytes 8 | tf_op jit(solution)/shard_map/psum | solution.py:60
  899.6 14.7 %all-gather.1 = bf16[512,512]{1,0:T(8,128)(2,1)S(1)} all-gather(bf16[64,512]{1,0:T(8,128)(2,1)S(1)} %fusion.17), channel_id=3, replica_groups=mesh['dp'=64,'tensor'=8] {'tensor'}, dimensions={0}, use_global_device_ids=true | all-gather | bytes 589824 | tf_op jit(solution)/shard_map/all_gather | solution.py:63
  914.3 1.2 bitcast_multiply_fusion
  915.4 14.9 %all-to-all-start.1 = ((bf16[1,64,16,512]{3,2,0,1:T(8,128)(2,1)}), bf16[1,64,16,512]{3,2,0,1:T(8,128)(2,1)S(1)}, u32[]{:S(2)}, u32[]{:S(2)}) async-start(bf16[1,64,16,512]{3,2,0,1:T(8,128)(2,1)} %bitcast_multiply_fusion), calls=%async_computation.2 | async-start | bytes 2097152 | tf_op jit(solution)/shard_map/all_to_all | solution.py:74
  930.4 0.0 copy-done.3
  930.4 0.0 copy-done.1
  930.4 1.8 fusion.1
  932.2 0.0 copy-done.4
  932.2 1.4 fusion.3
  933.6 47.4 %all-to-all-done.1 = bf16[1,64,16,512]{3,2,0,1:T(8,128)(2,1)S(1)} async-done(((bf16[1,64,16,512]{3,2,0,1:T(8,128)(2,1)}), bf16[1,64,16,512]{3,2,0,1:T(8,128)(2,1)S(1)}, u32[]{:S(2)}, u32[]{:S(2)}) %all-to-all-start.1) | async-done | bytes 1048608 | tf_op jit(solution)/shard_map/all_to_all | solution.py:74
  981.0 0.7 convolution_convert_fusion
  981.6 0.6 copy.28
  (4 shorter events, 0.0 us)
Async XLA Ops:
  7.2 876.0 %copy-start = (f32[1,64,512]{2,1,0:T(8,128)S(1)}, f32[1,64,512]{2,1,0:T(8,128)}, u32[]{:S(2)}) copy-start(f32[1,64,512]{2,1,0:T(8,128)} %param.11) | copy-start | bytes 393220
  7.2 704.6 %reduce-scatter.2.cloned.1.call-start = ((), (), s32[]{:S(2)}) async-start(), calls=%async_computation.3 | async-start | bytes 4259840 | tf_op jit(solution)/shard_map/reduce_scatter | solution.py:32
  17.5 694.4 %copy-start.5 = (s32[64,1]{0,1:T(1,128)S(1)}, s32[64,1]{0,1:T(1,128)}, u32[]{:S(2)}) copy-start(s32[64,1]{0,1:T(1,128)} %param.13) | copy-start | bytes 772
  17.5 829.8 %copy-start.2 = (f32[1,64,512]{2,1,0:T(8,128)S(1)}, f32[1,64,512]{2,1,0:T(8,128)}, u32[]{:S(2)}) copy-start(f32[1,64,512]{2,1,0:T(8,128)} %param.12) | copy-start | bytes 393220
  17.5 829.8 %all-reduce.2.cloned.1.call-start = ((), (), s32[]{:S(2)}) async-start(), calls=%async_computation.4 | async-start | bytes 2097152 | tf_op jit(solution)/shard_map/psum | solution.py:42
  762.7 167.7 %copy-start.3 = (f32[1,64,512]{2,1,0:T(8,128)S(1)}, f32[1,64,512]{2,1,0:T(8,128)}, u32[]{:S(2)}) copy-start(f32[1,64,512]{2,1,0:T(8,128)} %param.9) | copy-start | bytes 393220
  762.7 120.5 %all-gather.4.cloned.1.call-start = ((), (), s32[]{:S(2)}) async-start(), calls=%async_computation.5 | async-start | bytes 1179648 | tf_op jit(solution)/shard_map/all_gather | solution.py:55
  847.3 83.1 %copy-start.1 = (f32[1,512,512]{2,1,0:T(8,128)S(1)}, f32[1,512,512]{2,1,0:T(8,128)}, u32[]{:S(2)}) copy-start(f32[1,512,512]{2,1,0:T(8,128)} %all-reduce.2.cloned.1.call-done) | copy-start | bytes 3145732
  850.4 81.8 %copy-start.4 = (f32[1,64,512]{2,1,0:T(8,128)S(1)}, f32[1,64,512]{2,1,0:T(8,128)}, u32[]{:S(2)}) copy-start(f32[1,64,512]{2,1,0:T(8,128)} %param.10) | copy-start | bytes 393220
  915.4 65.5 %all-to-all-start.1 = ((bf16[1,64,16,512]{3,2,0,1:T(8,128)(2,1)}), bf16[1,64,16,512]{3,2,0,1:T(8,128)(2,1)S(1)}, u32[]{:S(2)}, u32[]{:S(2)}) async-start(bf16[1,64,16,512]{3,2,0,1:T(8,128)(2,1)} %bitcast_multiply_fusion), calls=%async_computation.2 | async-start | bytes 2097152 | tf_op jit(solution)/shard_map/all_to_all | solution.py:74
Sparse Core Ops, SparseCore 0:
  17.6 694.1 reduce-scatter.1
  762.8 84.4 all-reduce.1
  850.5 32.6 all-gather.3
where the time goes:
time: 992 us; the launch traced here: 989 us
  waiting for transfers between devices  853 us (86%)
  blocking collectives  76 us (8%)
  between operations  17.9 us (2%)
  matrix products  15.2 us (2%)
  starting transfers between devices  15 us (2%)
    reduce_scatter x1, waiting for transfers between devices, on_device(): lax.psum_scatter(gram_contribution.reshape(lax.axis_size('dp') * rows_per...  694 us
    psum x1, waiting for transfers between devices, on_device(): owned = lax.psum(incoming.reshape(CAP, BLK, BLK), 'tensor')  84.5 us
    all_to_all x1, blocking collectives, on_device(): lax.all_to_all(outgoing, 'dp', split_axis=1, concat_axis=1, tiled=True)  48.7 us
    all_to_all x1, waiting for transfers between devices, on_device(): lax.all_to_all(outgoing_back, 'dp', split_axis=1, concat_axis=1, tiled=True)  47.4 us
    all_gather x1, waiting for transfers between devices, on_device(): lax.all_gather(turned, 'tensor', axis=1, tiled=True)  26.6 us
  transfers between devices with their start and end apart: 4, of which 4 were waited for; matrix products, arithmetic and copies ran while one was open for 1% of the time, Pallas kernels for 0%

commit v1 on v0

v1 whole, which is shorter than its diff:
```python
import functools

import jax
import jax.numpy as jnp
from jax import lax
from jax.experimental import pallas as pl
from jax.experimental.pallas import tpu as pltpu
from jax.sharding import PartitionSpec as P

BLK = 512
NX = 4
NY = 4
NZ = 16
NT = 8
NB = 32
FACTOR_DECAY = 0.9
GRAFT_EPSILON = 1e-06
MESH = pl.DeviceIdType.MESH
F32 = jnp.float32
BF16 = jnp.bfloat16

NN = (((1,), (0,)), ((), ()))
NTR = (((1,), (1,)), ((), ()))
TN = (((0,), (0,)), ((), ()))


def dot(a, b, dims):
    return lax.dot_general(a, b, dims, preferred_element_type=F32)


def split(a):
    hi = a.astype(BF16)
    return hi, (a - hi.astype(F32)).astype(BF16)


def dot3(a, b, dims):
    return dot(a[0], b[0], dims) + (dot(a[0], b[1], dims) + dot(a[1], b[0], dims))


def loop(low, high, body):
    def step(k, carry):
        body(k)
        return carry

    lax.fori_loop(low, high, step, 0)


def kernel(
    x_ref, g_ref, ls_ref, rs_ref, lr_ref, rr_ref, ob_ref,
    ln_ref, rn_ref, dir_ref,
    xown, xb1, xb2, xb3, gown, gb1, gb2, gb3, part, ring_m, ring_p, own, r1, sb, hrel, lh, rrb, hhi, hlo, lsv, rsv, lgram,
    sq, sq_own, upd, fbuf, sb2, gr, zsel, xsel,
    loc, xs, xr, ys, yr, ds_, dr, gs, gr_s, lsd, lrv, rrs, rrr,
    rms, rmr, rps, rpr, a_s, a_r, b_s, b_r, c_s, c_r, cd_s, cd_r, e_s, e_r, f_s, f_r, h_s, h_r,
):
    d = lax.axis_index("dp")
    t = lax.axis_index("tensor")
    x = d // NZ
    z = d % NZ
    y = t // 2
    c = t % 2
    sib = y * 2 + (1 - c)

    def rc(src, dst, ssem, rsem, dx, dz, dt):
        return pltpu.make_async_remote_copy(
            src_ref=src, dst_ref=dst, send_sem=ssem, recv_sem=rsem,
            device_id=(dx * NZ + dz, dt), device_id_type=MESH,
        )

    local = [
        pltpu.make_async_copy(x_ref, xown, loc.at[0]),
        pltpu.make_async_copy(g_ref.at[:, pl.ds(pl.multiple_of(x * 128, 128), 128)], gown.at[0], loc.at[1]),
        pltpu.make_async_copy(g_ref.at[:, pl.ds(pl.multiple_of(512 + x * 128, 128), 128)], gown.at[1], loc.at[2]),
        pltpu.make_async_copy(rr_ref.at[0], rrb.at[c], loc.at[3]),
        pltpu.make_async_copy(ls_ref.at[0], lsv, loc.at[4]),
        pltpu.make_async_copy(rs_ref.at[0], rsv, loc.at[5]),
    ]
    for copy in local:
        copy.start()

    barrier = pltpu.get_barrier_semaphore()

    def greet_slab(k):
        pl.semaphore_signal(
            barrier, inc=1, device_id=(((x + k // NT) % NX) * NZ + z, (t + k % NT) % NT), device_id_type=MESH
        )

    def greet_ring(k):
        pl.semaphore_signal(barrier, inc=1, device_id=(x * NZ + (z + k) % NZ, t), device_id_type=MESH)

    loop(1, NX * NT, greet_slab)
    loop(1, NZ, greet_ring)
    pl.semaphore_wait(barrier, NX * NT - 1 + NZ - 1)

    order = (1, 3, 2)
    xb = (xown, xb1, xb2, xb3)
    gb = (gown, gb1, gb2, gb3)

    def x_copy(i):
        return rc(x_ref.at[y, c], xb[NX - i].at[0, 0], xs.at[i], xr.at[NX - i], (x + i) % NX, z, t)

    def g_copy(cb, i):
        to = (x + i) % NX
        columns = pl.ds(pl.multiple_of(cb * BLK + to * 128, 128), 128)
        return rc(g_ref.at[:, columns], gb[NX - i].at[cb], gs.at[cb, i], gr_s.at[cb, NX - i], to, z, t)

    x_send = [x_copy(i) for i in order]
    g_send = [g_copy(cb, i) for cb in range(2) for i in order]
    for copy in x_send + g_send:
        copy.start()

    rr_send = rc(rr_ref.at[0], rrb.at[c], rrs, rrr, x, z, sib)
    rr_send.start()
    l_core = y // 2
    l_self = l_core == c
    l_local = pltpu.make_async_copy(lr_ref.at[0], lh.at[t % 4], loc.at[6])

    def l_send(j):
        return rc(lr_ref.at[0], lh.at[t % 4], lsd.at[j], lrv.at[t % 4], x, z, ((y + j) % NY) * 2 + l_core)

    pl.when(l_self)(lambda: l_local.start())
    pl.when(jnp.logical_not(l_self))(lambda: l_send(0).start())
    for j in range(1, NY):
        l_send(j).start()

    def y_copy(i, j):
        to = ((y + j) % NY) * 2 + c
        return rc(xb[i].at[0, 0], xb[i].at[NY - j, 0], ys.at[i, j], yr.at[i, NY - j], x, z, to)

    def core_copy(i, j):
        return rc(xb[i].at[j, 0], xb[i].at[j, 1], ds_.at[i, j], dr.at[i, j], x, z, sib)

    y_send, d_send = [], []
    for i in order:
        x_copy(NX - i).wait_recv()
        for j in order:
            y_send.append(y_copy(i, j))
            y_send[-1].start()
        d_send.append(core_copy(i, 0))
        d_send[-1].start()

    def find_z(b):
        def step(k, found):
            return jnp.where(ob_ref[x * NZ + k] == b, k, found)

        zsel[b] = lax.fori_loop(0, NZ, step, 0)

    loop(0, NB, find_z)
    for cb in range(2):
        wanted = t * 4 + (x // 2) * 2 + cb

        def step(k, found):
            return jnp.where(ob_ref[k] == wanted, k // NZ, found)

        xsel[cb] = lax.fori_loop(0, NX * NZ, step, 0)

    for copy in local[:3]:
        copy.wait()

    def gram(act, grads):
        return [dot(grads[cb], act, TN).reshape(NZ, 8, 1024) for cb in range(2)]

    for cb, value in enumerate(gram(xown[...].reshape(256, 1024), gown)):
        part[cb] = value

    for i in order:
        for j in (3, 1, 2):
            y_copy(i, NY - j).wait_recv()
            d_send.append(core_copy(i, j))
            d_send[-1].start()
    for i in order:
        for j in range(NY):
            core_copy(i, j).wait_recv()
        for cb in range(2):
            g_copy(cb, NX - i).wait_recv()
        act = jnp.concatenate(
            [xb[i][(row + NY - y) % NY, (core + c) % 2] for row in range(NY) for core in range(2)], axis=0
        )
        for cb, value in enumerate(gram(act, gb[i])):
            part[cb] += value

    up, down = (z + 1) % NZ, (z + NZ - 1) % NZ

    def minus(cb, s, src):
        return rc(src, ring_m.at[cb, s], rms.at[cb, s], rmr.at[cb, s], x, down, t)

    def plus(cb, s, src):
        return rc(src, ring_p.at[cb, s], rps.at[cb, s], rpr.at[cb, s], x, up, t)

    for cb in range(2):
        minus(cb, 0, part.at[cb, (z + 8) % NZ]).start()
        plus(cb, 0, part.at[cb, (z + 7) % NZ]).start()

    for s in range(1, 8):
        for cb in range(2):
            minus(cb, s - 1, part.at[cb, 0]).wait_recv()
            ring_m[cb, s - 1] = ring_m[cb, s - 1] + part[cb, (z + 8 + s) % NZ]
            minus(cb, s, ring_m.at[cb, s - 1]).start()
            if s < 7:
                plus(cb, s - 1, part.at[cb, 0]).wait_recv()
                ring_p[cb, s - 1] = ring_p[cb, s - 1] + part[cb, (z + 7 - s) % NZ]
                plus(cb, s, ring_p.at[cb, s - 1]).start()
    for cb in range(2):
        plus(cb, 6, part.at[cb, 0]).wait_recv()
        minus(cb, 7, part.at[cb, 0]).wait_recv()
        total = part[cb, z] + (ring_p[cb, 6] + ring_m[cb, 7])
        for rb in range(2):
            for row in range(NY):
                low = rb * BLK + row * 128
                own[row, rb, cb] = total[:, low : low + 128]

    a_core = x // 2

    def a_copy(k):
        to_x, to_y = (x + k // NY) % NX, (y + k % NY) % NY
        return own.at[to_y], to_x, to_y * 2 + a_core

    def a_send(k):
        src, to_x, to_t = a_copy(k)
        return rc(src, r1.at[t, x % 2], a_s.at[k], a_r.at[t, x % 2], to_x, z, to_t)

    a_local = pltpu.make_async_copy(a_copy(0)[0], r1.at[t, x % 2], loc.at[7])
    a_self = a_core == c
    pl.when(a_self)(lambda: a_local.start())
    pl.when(jnp.logical_not(a_self))(lambda: a_send(0).start())
    loop(1, 16, lambda k: a_send(k).start())
    pl.when(a_self)(lambda: a_local.wait())

    def a_wait(k):
        from_t, half = k // 2, k % 2
        from_x = c * 2 + half

        @pl.when(jnp.logical_or(from_t != t, from_x != x))
        def _():
            piece = r1.at[from_t, half]
            rc(piece, piece, a_s.at[0], a_r.at[from_t, half], from_x, z, from_t).wait_recv()

    loop(0, 16, a_wait)

    def b_fill(k):
        block = ob_ref[x * NZ + k]
        safe = jnp.minimum(block, NB - 1)
        for half in range(2):
            value = r1[safe // 4, half, (safe // 2) % 2, safe % 2]
            sb[k, half] = jnp.where(block < NB, value, jnp.zeros_like(value))

    def b_send(k):
        to = (z + k) % NZ
        return rc(sb.at[to], hrel.at[0, 0, z], b_s.at[k], b_r.at[z], x, to, t)

    loop(0, NZ, b_fill)
    loop(1, NZ, lambda k: b_send(k).start())
    b_local = pltpu.make_async_copy(sb.at[z], hrel.at[0, 0, z], loc.at[9])
    b_local.start()

    def b_wait(k):
        src = (z + k) % NZ
        rc(sb.at[0], hrel.at[0, 0, src], b_s.at[0], b_r.at[src], x, src, t).wait_recv()

    loop(1, NZ, b_wait)
    b_local.wait()

    def c_copy(j):
        return rc(
            hrel.at[0, 0], hrel.at[0, NY - j], c_s.at[j], c_r.at[NY - j], x, z, ((y + j) % NY) * 2 + c
        )

    def cd_copy(j):
        return rc(hrel.at[0, j], hrel.at[1, j], cd_s.at[j], cd_r.at[j], x, z, sib)

    c_send = [c_copy(j) for j in order]
    for copy in c_send:
        copy.start()
    cd_send = [cd_copy(j) for j in (0, 1, 3, 2)]
    for j, copy in zip((0, 1, 3, 2), cd_send):
        if j > 0:
            c_copy(NY - j).wait_recv()
        copy.start()
    for copy in cd_send:
        copy.wait_recv()

    local[3].wait()
    rc(rrb.at[1 - c], rrb.at[1 - c], rrs, rrr, x, z, sib).wait_recv()
    pl.when(l_self)(lambda: l_local.wait())

    def l_wait(k):
        from_t = c * 4 + k

        @pl.when(from_t != t)
        def _():
            rc(lh.at[k], lh.at[k], lsd.at[0], lrv.at[k], x, z, from_t).wait_recv()

    loop(0, 4, l_wait)
    h = jnp.concatenate(
        [
            jnp.concatenate([hrel[(half // 2 + c) % 2, (row + NY - y) % NY, :, half % 2].reshape(128, 128) for half in range(NX)], axis=0)
            for row in range(NY)
        ],
        axis=1,
    )
    hi, lo = split(h)
    hhi[...] = hi
    hlo[...] = lo
    grad_square = jnp.sum(h * h) / (BLK * BLK)
    h2 = (hi, lo)
    turned = dot3(split(rrb[...].reshape(128, BLK)), h2, NN)
    precond = dot3(split(lh[...].reshape(256, BLK)), split(turned), NTR)
    sq_own[...] = jnp.sum((precond * precond).reshape(32, 8, 128), axis=0)

    def e_copy(k):
        return rc(sq_own, sq.at[NT - 1 - k], e_s.at[k], e_r.at[NT - k], x, z, (t + k) % NT)

    for k in range(1, NT):
        e_copy(k).start()

    fraction = (1.0 - FACTOR_DECAY) / BLK
    rows = pl.ds(pl.multiple_of(t * 64, 64), 64)
    local[5].wait()
    right = dot3((hhi[rows, :], hlo[rows, :]), h2, NTR)
    rn_ref[0] = FACTOR_DECAY * rsv[...] + fraction * right

    for k in range(1, NT):
        e_copy(k).wait_recv()
    prec_square = (jnp.sum(sq[...]) + jnp.sum(sq_own[...])) / (BLK * BLK)
    graft = jnp.sqrt(jnp.full((1, 128), (grad_square + GRAFT_EPSILON) / (prec_square + GRAFT_EPSILON), F32))
    upd[...] = (precond * graft).astype(BF16).reshape(NZ, 16, 128)

    def f_send(k):
        to = (z + k) % NZ
        return rc(upd.at[to], fbuf.at[z], f_s.at[k], f_r.at[z], x, to, t)

    loop(1, NZ, lambda k: f_send(k).start())
    f_local = pltpu.make_async_copy(upd.at[z], fbuf.at[z], loc.at[10])
    f_local.start()

    local[4].wait()
    lanes = pl.ds(pl.multiple_of(y * 128, 128), 128)
    left = dot3((hhi[:, lanes], hlo[:, lanes]), h2, TN)
    lgram[...] = left.reshape(2, 64, BLK)
    ln_ref[0] = FACTOR_DECAY * lsv[...] + fraction * lgram[c]

    def f_wait(k):
        src = (z + k) % NZ
        rc(fbuf.at[src], fbuf.at[src], f_s.at[k], f_r.at[src], x, src, t).wait_recv()

    loop(1, NZ, f_wait)
    f_local.wait()

    def h_fill(k):
        rb, to_t = k // NT, k % NT
        for cb in range(2):
            sb2[k, cb] = fbuf[zsel[to_t * 4 + rb * 2 + cb]]

    def h_is_self(k):
        return jnp.logical_and(c + 2 * (k // NT) == x, k % NT == t)

    def h_send(k):
        return rc(sb2.at[k], gr.at[x, y], h_s.at[k], h_r.at[x, y], c + 2 * (k // NT), z, k % NT)

    def h_start(k):
        pl.when(h_is_self(k))(lambda: pltpu.make_async_copy(sb2.at[k], gr.at[x, y], loc.at[8]).start())
        pl.when(jnp.logical_not(h_is_self(k)))(lambda: h_send(k).start())

    loop(0, 16, h_fill)
    loop(0, 16, h_start)

    def h_wait(k):
        from_x, from_y = k // NY, k % NY
        from_t = from_y * 2 + x % 2
        same = jnp.logical_and(from_x == x, from_t == t)
        place = gr.at[from_x, from_y]
        pl.when(same)(lambda: pltpu.make_async_copy(place, place, loc.at[8]).wait())
        pl.when(jnp.logical_not(same))(
            lambda: rc(place, place, h_s.at[0], h_r.at[from_x, from_y], from_x, z, from_t).wait_recv()
        )

    loop(0, 16, h_wait)
    for cb in range(2):
        for row in range(NY):
            dir_ref[:, cb * BLK + row * 128 : cb * BLK + (row + 1) * 128] = gr[xsel[cb], row, cb]

    for copy in x_send + g_send + y_send + d_send + c_send + cd_send + [rr_send]:
        copy.wait_send()
    pl.when(jnp.logical_not(l_self))(lambda: l_send(0).wait_send())
    for j in range(1, NY):
        l_send(j).wait_send()

    for s in range(8):
        for cb in range(2):
            minus(cb, s, part.at[cb, 0]).wait_send()
            if s < 7:
                plus(cb, s, part.at[cb, 0]).wait_send()
    pl.when(jnp.logical_not(a_self))(lambda: a_send(0).wait_send())
    loop(1, 16, lambda k: a_send(k).wait_send())
    loop(1, NZ, lambda k: b_send(k).wait_send())
    for k in range(1, NT):
        e_copy(k).wait_send()
    loop(1, NZ, lambda k: f_send(k).wait_send())
    loop(0, 16, lambda k: pl.when(jnp.logical_not(h_is_self(k)))(lambda: h_send(k).wait_send()))


def on_device(inputs, out_grad, left_stat, right_stat, left_root, right_root, owner_blocks):
    anywhere = pl.BlockSpec(memory_space=pltpu.HBM)
    in_vmem = pl.BlockSpec(memory_space=pltpu.VMEM)
    dma = pltpu.SemaphoreType.DMA
    return pl.pallas_call(
        kernel,
        out_shape=(
            jax.ShapeDtypeStruct((1, 64, BLK), F32),
            jax.ShapeDtypeStruct((1, 64, BLK), F32),
            jax.ShapeDtypeStruct((16, 1024), BF16),
        ),
        in_specs=[anywhere] * 6 + [pl.BlockSpec(memory_space=pltpu.SMEM)],
        out_specs=(in_vmem, in_vmem, in_vmem),
        scratch_shapes=[
            pltpu.VMEM((NY, 2, 32, 1024), BF16),
            pltpu.VMEM((NY, 2, 32, 1024), BF16),
            pltpu.VMEM((NY, 2, 32, 1024), BF16),
            pltpu.VMEM((NY, 2, 32, 1024), BF16),
            pltpu.VMEM((2, 256, 128), BF16),
            pltpu.VMEM((2, 256, 128), BF16),
            pltpu.VMEM((2, 256, 128), BF16),
            pltpu.VMEM((2, 256, 128), BF16),
            pltpu.VMEM((2, NZ, 8, 1024), F32),
            pltpu.VMEM((2, 8, 8, 1024), F32),
            pltpu.VMEM((2, 7, 8, 1024), F32),
            pltpu.VMEM((NY, 2, 2, 8, 128), F32),
            pltpu.VMEM((NT, 2, 2, 2, 8, 128), F32),
            pltpu.VMEM((NZ, 2, 8, 128), F32),
            pltpu.VMEM((2, NY, NZ, 2, 8, 128), F32),
            pltpu.VMEM((4, 64, BLK), F32),
            pltpu.VMEM((2, 64, BLK), F32),
            pltpu.VMEM((BLK, BLK), BF16),
            pltpu.VMEM((BLK, BLK), BF16),
            pltpu.VMEM((64, BLK), F32),
            pltpu.VMEM((64, BLK), F32),
            pltpu.VMEM((2, 64, BLK), F32),
            pltpu.VMEM((NT - 1, 8, 128), F32),
            pltpu.VMEM((8, 128), F32),
            pltpu.VMEM((NZ, 16, 128), BF16),
            pltpu.VMEM((NZ, 16, 128), BF16),
            pltpu.VMEM((16, 2, 16, 128), BF16),
            pltpu.VMEM((NX, NY, 2, 16, 128), BF16),
            pltpu.SMEM((NB,), jnp.int32),
            pltpu.SMEM((2,), jnp.int32),
            dma((11,)),
            dma((4,)), dma((4,)),
            dma((4, 4)), dma((4, 4)),
            dma((4, 4)), dma((4, 4)),
            dma((2, 4)), dma((2, 4)),
            dma((4,)), dma((4,)),
            dma, dma,
            dma((2, 8)), dma((2, 8)), dma((2, 7)), dma((2, 7)),
            dma((16,)), dma((8, 2)),
            dma((16,)), dma((16,)),
            dma((4,)), dma((4,)), dma((4,)), dma((4,)),
            dma((8,)), dma((8,)),
            dma((16,)), dma((16,)),
            dma((16,)), dma((4, 4)),
        ],
        compiler_params=pltpu.CompilerParams(
            collective_id=0, has_side_effects=True, vmem_limit_bytes=40 * 1024 * 1024
        ),
        name="shampoo",
    )(
        inputs.reshape(NY, 2, 32, 1024), out_grad, left_stat, right_stat, left_root, right_root,
        owner_blocks.reshape(NX * NZ),
    )


def solution(mesh):
    placed = (
        P("dp", None),
        P("dp", "tensor"),
        P("dp", "tensor", None),
        P("dp", "tensor", None),
        P("dp", "tensor", None),
        P("dp", "tensor", None),
        P(),
    )
    return jax.shard_map(
        on_device,
        mesh=mesh,
        in_specs=placed,
        out_specs=(P("dp", "tensor", None), P("dp", "tensor", None), P("dp", "tensor")),
        check_vma=False,
    )
```

time: 992 us -> 119 us (0.12)
  waiting for transfers between devices: 853 us -> 0 us
  Pallas kernels: 0 us -> 109 us
  blocking collectives: 76 us -> 0 us
  between operations: 17.9 us -> 0.66 us
  matrix products: 15.2 us -> 0 us
  starting transfers between devices: 15 us -> 0 us
    reduce_scatter x1 -> x0, waiting for transfers between devices: 694 us -> none  [on_device(): lax.psum_scatter(gram_contribution.reshape(lax.axis_size('dp') * rows_per...]
    pallas_call x0 -> x1, Pallas kernels: none -> 109 us  [on_device(): pl.pallas_call(kernel, out_shape=(jax.ShapeDtypeStruct((1, 64, BLK), F32)...]
    psum x1 -> x0, waiting for transfers between devices: 84.5 us -> none  [on_device(): owned = lax.psum(incoming.reshape(CAP, BLK, BLK), 'tensor')]
    all_to_all x1 -> x0, blocking collectives: 48.7 us -> none  [on_device(): lax.all_to_all(outgoing, 'dp', split_axis=1, concat_axis=1, tiled=True)]
    all_to_all x1 -> x0, waiting for transfers between devices: 47.4 us -> none  [on_device(): lax.all_to_all(outgoing_back, 'dp', split_axis=1, concat_axis=1, tiled=True)]
    all_gather x1 -> x0, waiting for transfers between devices: 26.6 us -> none  [on_device(): lax.all_gather(turned, 'tensor', axis=1, tiled=True)]
    dot_general x7 -> x0, matrix products: 15.2 us -> none  [the longest x1 3.72 us: on_device(): jnp.einsum('osz,ofx->zsfx', input_activations, output_gradients, preferre...]
    all_to_all x1 -> x0, starting transfers between devices: 14.9 us -> none  [on_device(): lax.all_to_all(outgoing_back, 'dp', split_axis=1, concat_axis=1, tiled=True)]
  transfers between devices with their start and end apart: 4 -> 0, of which waited for: 4 -> 0; matrix products, arithmetic and copies ran while one was open for 1% -> 0% of each run, Pallas kernels for 0% -> 0%
where the time goes in v1:
time: 119 us; the launch traced here: 118 us
  Pallas kernels  109 us (92%)
  local copies, waits for them, and re-layouts  8.27 us (7%)
    pallas_call x1, Pallas kernels, on_device(): pl.pallas_call(kernel, out_shape=(jax.ShapeDtypeStruct((1, 64, BLK), F32)...  109 us
    unnamed x17, local copies, waits for them, and re-layouts  8.27 us

profile of v1, /device:TPU:1, one launch (start us, length us, event | category | flops | bytes accessed | tf_op | source)
XLA Modules:
  0.0 118.3 jit_solution(10966051424895013906)
XLA Ops:
  0.6 0.0 copy-start.6
  0.6 0.6 copy-done.6
  1.3 0.0 copy-start
  1.3 1.0 copy-done
  2.3 0.0 copy-start.1
  2.3 1.0 copy-done.1
  3.4 0.0 copy-start.2
  3.4 0.9 copy-done.2
  4.3 0.0 copy-start.3
  4.3 0.9 copy-done.3
  5.2 0.0 copy-start.4
  5.2 0.9 copy-done.4
  6.1 0.0 copy-start.5
  6.1 0.9 copy-done.5
  7.0 109.4 %shampoo.1 = (f32[1,64,512]{2,1,0:T(8,128)S(1)}, f32[1,64,512]{2,1,0:T(8,128)S(1)}, bf16[16,1024]{1,0:T(8,128)(2,1)S(1)}) custom-call(bf16[4,2,32,1024]{3,2,1,0:T(8,128)(2,1)S(1)} %bitcast.2, bf16[256,1024]{1,0:T(8,128)(2,1)S(1)} %copy-done.1, f32[1,64,512]{2,1,0:T(8,128)S(1)} %copy-done.2, f32[1,64,512]{2,1,0:T(8,128)S(1)} %copy-done.3, ...), custom_call_target="tpu_custom_call" | custom-call | tf_op jit(solution)/shard_map/shampoo/pallas_call | solution.py:406
  116.4 0.7 copy.13
  117.1 0.7 copy.14
  117.7 0.6 copy.15
Async XLA Ops:
  0.6 0.7 copy-start.6
  1.3 1.0 copy-start
  2.3 1.0 copy-start.1
  3.4 0.9 copy-start.2
  4.3 0.9 copy-start.3
  5.2 0.9 copy-start.4
  6.1 0.9 copy-start.5

commit v2 on v1

--- a/solution.py
+++ b/solution.py
@@ -79,49 +79,41 @@
         copy.start()
 
     barrier = pltpu.get_barrier_semaphore()
-
-    def greet_slab(k):
-        pl.semaphore_signal(
-            barrier, inc=1, device_id=(((x + k // NT) % NX) * NZ + z, (t + k % NT) % NT), device_id_type=MESH
-        )
-
-    def greet_ring(k):
-        pl.semaphore_signal(barrier, inc=1, device_id=(x * NZ + (z + k) % NZ, t), device_id_type=MESH)
-
-    loop(1, NX * NT, greet_slab)
-    loop(1, NZ, greet_ring)
-    pl.semaphore_wait(barrier, NX * NT - 1 + NZ - 1)
+    met = [((x + i) % NX, z, t) for i in (1, 3, 2)] + [(x, z, (t + k) % NT) for k in range(1, NT)]
+    met += [(x, (z + k) % NZ, t) for k in (1, NZ - 1)]
+    for to_x, to_z, to_t in met:
+        pl.semaphore_signal(barrier, inc=1, device_id=(to_x * NZ + to_z, to_t), device_id_type=MESH)
+    pl.semaphore_wait(barrier, len(met))
 
     order = (1, 3, 2)
     xb = (xown, xb1, xb2, xb3)
     gb = (gown, gb1, gb2, gb3)
 
-    def x_copy(i):
-        return rc(x_ref.at[y, c], xb[NX - i].at[0, 0], xs.at[i], xr.at[NX - i], (x + i) % NX, z, t)
+    def x_copy(i, j):
+        src = x_ref.at[(y + j) % NY, c]
+        return rc(src, xb[NX - i].at[j, 0], xs.at[i, j], xr.at[NX - i, j], (x + i) % NX, z, t)
 
     def g_copy(cb, i):
         to = (x + i) % NX
         columns = pl.ds(pl.multiple_of(cb * BLK + to * 128, 128), 128)
         return rc(g_ref.at[:, columns], gb[NX - i].at[cb], gs.at[cb, i], gr_s.at[cb, NX - i], to, z, t)
 
-    x_send = [x_copy(i) for i in order]
+    x_send = [x_copy(i, j) for j in (0, 2) for i in order]
     g_send = [g_copy(cb, i) for cb in range(2) for i in order]
     for copy in x_send + g_send:
         copy.start()
 
-    rr_send = rc(rr_ref.at[0], rrb.at[c], rrs, rrr, x, z, sib)
-    rr_send.start()
-    l_core = y // 2
-    l_self = l_core == c
-    l_local = pltpu.make_async_copy(lr_ref.at[0], lh.at[t % 4], loc.at[6])
-
-    def l_send(j):
-        return rc(lr_ref.at[0], lh.at[t % 4], lsd.at[j], lrv.at[t % 4], x, z, ((y + j) % NY) * 2 + l_core)
-
-    pl.when(l_self)(lambda: l_local.start())
-    pl.when(jnp.logical_not(l_self))(lambda: l_send(0).start())
-    for j in range(1, NY):
-        l_send(j).start()
+    for copy in local[:3]:
+        copy.wait()
+
+    def gram(act, grads):
+        value = dot(jnp.concatenate([grads[0], grads[1]], axis=1), act, TN)
+        for cb in range(2):
+            for rb in range(2):
+                yield cb, rb, value[cb * 128 : cb * 128 + 128, rb * BLK : rb * BLK + BLK].reshape(NZ, 8, BLK)
+
+    for cb, rb, value in gram(xown[...].reshape(256, 1024), gown):
+        part[cb, rb] = value
 
     def y_copy(i, j):
         to = ((y + j) % NY) * 2 + c
@@ -132,40 +124,19 @@
 
     y_send, d_send = [], []
     for i in order:
-        x_copy(NX - i).wait_recv()
-        for j in order:
+        x_copy(NX - i, 0).wait_recv()
+        for j in (1, 3):
             y_send.append(y_copy(i, j))
             y_send[-1].start()
         d_send.append(core_copy(i, 0))
         d_send[-1].start()
 
-    def find_z(b):
-        def step(k, found):
-            return jnp.where(ob_ref[x * NZ + k] == b, k, found)
-
-        zsel[b] = lax.fori_loop(0, NZ, step, 0)
-
-    loop(0, NB, find_z)
-    for cb in range(2):
-        wanted = t * 4 + (x // 2) * 2 + cb
-
-        def step(k, found):
-            return jnp.where(ob_ref[k] == wanted, k // NZ, found)
-
-        xsel[cb] = lax.fori_loop(0, NX * NZ, step, 0)
-
-    for copy in local[:3]:
-        copy.wait()
-
-    def gram(act, grads):
-        return [dot(grads[cb], act, TN).reshape(NZ, 8, 1024) for cb in range(2)]
-
-    for cb, value in enumerate(gram(xown[...].reshape(256, 1024), gown)):
-        part[cb] = value
-
     for i in order:
-        for j in (3, 1, 2):
-            y_copy(i, NY - j).wait_recv()
+        for j in (2, 1, 3):
+            if j == 2:
+                x_copy(NX - i, 2).wait_recv()
+            else:
+                y_copy(i, NY - j).wait_recv()
             d_send.append(core_copy(i, j))
             d_send[-1].start()
     for i in order:
@@ -176,38 +147,52 @@
         act = jnp.concatenate(
             [xb[i][(row + NY - y) % NY, (core + c) % 2] for row in range(NY) for core in range(2)], axis=0
         )
-        for cb, value in enumerate(gram(act, gb[i])):
-            part[cb] += value
+        for cb, rb, value in gram(act, gb[i]):
+            part[cb, rb] += value
 
     up, down = (z + 1) % NZ, (z + NZ - 1) % NZ
 
-    def minus(cb, s, src):
-        return rc(src, ring_m.at[cb, s], rms.at[cb, s], rmr.at[cb, s], x, down, t)
-
-    def plus(cb, s, src):
-        return rc(src, ring_p.at[cb, s], rps.at[cb, s], rpr.at[cb, s], x, up, t)
-
-    for cb in range(2):
-        minus(cb, 0, part.at[cb, (z + 8) % NZ]).start()
-        plus(cb, 0, part.at[cb, (z + 7) % NZ]).start()
+    chunks = [(cb, rb) for cb in range(2) for rb in range(2)]
+
+    def minus(q, s, src):
+        return rc(src, ring_m.at[*q, s], rms.at[*q, s], rmr.at[*q, s], x, down, t)
+
+    def plus(q, s, src):
+        return rc(src, ring_p.at[*q, s], rps.at[*q, s], rpr.at[*q, s], x, up, t)
+
+    for q in chunks:
+        minus(q, 0, part.at[*q, (z + 8) % NZ]).start()
+        plus(q, 0, part.at[*q, (z + 7) % NZ]).start()
+
+    rr_send = rc(rr_ref.at[0], rrb.at[c], rrs, rrr, x, z, sib)
+    rr_send.start()
+    l_core = y // 2
+    l_self = l_core == c
+    l_local = pltpu.make_async_copy(lr_ref.at[0], lh.at[t % 4], loc.at[6])
+
+    def l_send(j):
+        return rc(lr_ref.at[0], lh.at[t % 4], lsd.at[j], lrv.at[t % 4], x, z, ((y + j) % NY) * 2 + l_core)
+
+    pl.when(l_self)(lambda: l_local.start())
+    pl.when(jnp.logical_not(l_self))(lambda: l_send(0).start())
+    for j in range(1, NY):
+        l_send(j).start()
 
     for s in range(1, 8):
-        for cb in range(2):
-            minus(cb, s - 1, part.at[cb, 0]).wait_recv()
-            ring_m[cb, s - 1] = ring_m[cb, s - 1] + part[cb, (z + 8 + s) % NZ]
-            minus(cb, s, ring_m.at[cb, s - 1]).start()
+        for q in chunks:
+            minus(q, s - 1, part.at[*q, 0]).wait_recv()
+            ring_m[*q, s - 1] = ring_m[*q, s - 1] + part[*q, (z + 8 + s) % NZ]
+            minus(q, s, ring_m.at[*q, s - 1]).start()
             if s < 7:
-                plus(cb, s - 1, part.at[cb, 0]).wait_recv()
-                ring_p[cb, s - 1] = ring_p[cb, s - 1] + part[cb, (z + 7 - s) % NZ]
-                plus(cb, s, ring_p.at[cb, s - 1]).start()
-    for cb in range(2):
-        plus(cb, 6, part.at[cb, 0]).wait_recv()
-        minus(cb, 7, part.at[cb, 0]).wait_recv()
-        total = part[cb, z] + (ring_p[cb, 6] + ring_m[cb, 7])
-        for rb in range(2):
-            for row in range(NY):
-                low = rb * BLK + row * 128
-                own[row, rb, cb] = total[:, low : low + 128]
+                plus(q, s - 1, part.at[*q, 0]).wait_recv()
+                ring_p[*q, s - 1] = ring_p[*q, s - 1] + part[*q, (z + 7 - s) % NZ]
+                plus(q, s, ring_p.at[*q, s - 1]).start()
+    for q in chunks:
+        plus(q, 6, part.at[*q, 0]).wait_recv()
+        minus(q, 7, part.at[*q, 0]).wait_recv()
+        total = part[*q, z] + (ring_p[*q, 6] + ring_m[*q, 7])
+        for row in range(NY):
+            own[row, q[1], q[0]] = total[:, row * 128 : row * 128 + 128]
 
     a_core = x // 2
 
@@ -237,6 +222,11 @@
 
     loop(0, 16, a_wait)
 
+    def slot_of(o):
+        return max(2 * o - 1, 0) if o <= 8 else 2 * NZ - 2 * o
+
+    offset_of = sorted(range(NZ), key=slot_of)
+
     def b_fill(k):
         block = ob_ref[x * NZ + k]
         safe = jnp.minimum(block, NB - 1)
@@ -244,38 +234,46 @@
             value = r1[safe // 4, half, (safe // 2) % 2, safe % 2]
             sb[k, half] = jnp.where(block < NB, value, jnp.zeros_like(value))
 
-    def b_send(k):
+    def b_copy(k):
         to = (z + k) % NZ
-        return rc(sb.at[to], hrel.at[0, 0, z], b_s.at[k], b_r.at[z], x, to, t)
+        return rc(sb.at[to], hrel.at[0, 0, slot_of(NZ - k)], b_s.at[k], b_r.at[NZ - k], x, to, t)
 
     loop(0, NZ, b_fill)
-    loop(1, NZ, lambda k: b_send(k).start())
-    b_local = pltpu.make_async_copy(sb.at[z], hrel.at[0, 0, z], loc.at[9])
+    b_local = pltpu.make_async_copy(sb.at[z], hrel.at[0, 0, 0], loc.at[9])
     b_local.start()
-
-    def b_wait(k):
-        src = (z + k) % NZ
-        rc(sb.at[0], hrel.at[0, 0, src], b_s.at[0], b_r.at[src], x, src, t).wait_recv()
-
-    loop(1, NZ, b_wait)
-    b_local.wait()
-
-    def c_copy(j):
-        return rc(
-            hrel.at[0, 0], hrel.at[0, NY - j], c_s.at[j], c_r.at[NY - j], x, z, ((y + j) % NY) * 2 + c
-        )
-
-    def cd_copy(j):
-        return rc(hrel.at[0, j], hrel.at[1, j], cd_s.at[j], cd_r.at[j], x, z, sib)
-
-    c_send = [c_copy(j) for j in order]
-    for copy in c_send:
-        copy.start()
-    cd_send = [cd_copy(j) for j in (0, 1, 3, 2)]
-    for j, copy in zip((0, 1, 3, 2), cd_send):
-        if j > 0:
-            c_copy(NY - j).wait_recv()
-        copy.start()
+    for o in offset_of[:0:-1]:
+        b_copy(NZ - o).start()
+
+    def c_copy(g, j):
+        src, dst = hrel.at[0, 0, pl.ds(4 * g, 4)], hrel.at[0, NY - j, pl.ds(4 * g, 4)]
+        return rc(src, dst, c_s.at[g, j], c_r.at[g, NY - j], x, z, ((y + j) % NY) * 2 + c)
+
+    def cd_copy(g, j):
+        src, dst = hrel.at[0, j, pl.ds(4 * g, 4)], hrel.at[1, j, pl.ds(4 * g, 4)]
+        return rc(src, dst, cd_s.at[g, j], cd_r.at[g, j], x, z, sib)
+
+    c_send, cd_send = [], []
+
+    def pass_on(g):
+        for j in (1, 3, 2):
+            c_copy(g, NY - j).wait_recv()
+            cd_copy(g, j).start()
+            cd_send.append(cd_copy(g, j))
+
+    for g in range(4):
+        for o in offset_of[4 * g : 4 * g + 4]:
+            if o == 0:
+                b_local.wait()
+            else:
+                b_copy(NZ - o).wait_recv()
+        for j in (1, 3, 2):
+            c_copy(g, j).start()
+            c_send.append(c_copy(g, j))
+        cd_copy(g, 0).start()
+        cd_send.append(cd_copy(g, 0))
+        if g > 0:
+            pass_on(g - 1)
+    pass_on(3)
     for copy in cd_send:
         copy.wait_recv()
 
@@ -291,12 +289,20 @@
             rc(lh.at[k], lh.at[k], lsd.at[0], lrv.at[k], x, z, from_t).wait_recv()
 
     loop(0, 4, l_wait)
+    def place(row):
+        o = (row + NZ - z) % NZ
+        return jnp.where(o <= 8, jnp.maximum(2 * o - 1, 0), 2 * NZ - 2 * o)
+
+    def tile(col_x, row_z, row):
+        return hrel[(col_x // 2 + c) % 2, (row + NY - y) % NY, place(row_z), col_x % 2]
+
     h = jnp.concatenate(
         [
-            jnp.concatenate([hrel[(half // 2 + c) % 2, (row + NY - y) % NY, :, half % 2].reshape(128, 128) for half in range(NX)], axis=0)
-            for row in range(NY)
+            jnp.concatenate([tile(col_x, row_z, row) for row in range(NY)], axis=1)
+            for col_x in range(NX)
+            for row_z in range(NZ)
         ],
-        axis=1,
+        axis=0,
     )
     hi, lo = split(h)
     hhi[...] = hi
@@ -339,6 +345,21 @@
     lgram[...] = left.reshape(2, 64, BLK)
     ln_ref[0] = FACTOR_DECAY * lsv[...] + fraction * lgram[c]
 
+    def find_z(b):
+        def step(k, found):
+            return jnp.where(ob_ref[x * NZ + k] == b, k, found)
+
+        zsel[b] = lax.fori_loop(0, NZ, step, 0)
+
+    loop(0, NB, find_z)
+    for cb in range(2):
+        wanted = t * 4 + (x // 2) * 2 + cb
+
+        def step(k, found):
+            return jnp.where(ob_ref[k] == wanted, k // NZ, found)
+
+        xsel[cb] = lax.fori_loop(0, NX * NZ, step, 0)
+
     def f_wait(k):
         src = (z + k) % NZ
         rc(fbuf.at[src], fbuf.at[src], f_s.at[k], f_r.at[src], x, src, t).wait_recv()
@@ -386,13 +407,14 @@
         l_send(j).wait_send()
 
     for s in range(8):
-        for cb in range(2):
-            minus(cb, s, part.at[cb, 0]).wait_send()
+        for q in chunks:
+            minus(q, s, part.at[*q, 0]).wait_send()
             if s < 7:
-                plus(cb, s, part.at[cb, 0]).wait_send()
+                plus(q, s, part.at[*q, 0]).wait_send()
     pl.when(jnp.logical_not(a_self))(lambda: a_send(0).wait_send())
     loop(1, 16, lambda k: a_send(k).wait_send())
-    loop(1, NZ, lambda k: b_send(k).wait_send())
+    for k in range(1, NZ):
+        b_copy(k).wait_send()
     for k in range(1, NT):
         e_copy(k).wait_send()
     loop(1, NZ, lambda k: f_send(k).wait_send())
@@ -421,9 +443,9 @@
             pltpu.VMEM((2, 256, 128), BF16),
             pltpu.VMEM((2, 256, 128), BF16),
             pltpu.VMEM((2, 256, 128), BF16),
-            pltpu.VMEM((2, NZ, 8, 1024), F32),
-            pltpu.VMEM((2, 8, 8, 1024), F32),
-            pltpu.VMEM((2, 7, 8, 1024), F32),
+            pltpu.VMEM((2, 2, NZ, 8, BLK), F32),
+            pltpu.VMEM((2, 2, 8, 8, BLK), F32),
+            pltpu.VMEM((2, 2, 7, 8, BLK), F32),
             pltpu.VMEM((NY, 2, 2, 8, 128), F32),
             pltpu.VMEM((NT, 2, 2, 2, 8, 128), F32),
             pltpu.VMEM((NZ, 2, 8, 128), F32),
@@ -444,22 +466,22 @@
             pltpu.SMEM((NB,), jnp.int32),
             pltpu.SMEM((2,), jnp.int32),
             dma((11,)),
-            dma((4,)), dma((4,)),
+            dma((4, 4)), dma((4, 4)),
             dma((4, 4)), dma((4, 4)),
             dma((4, 4)), dma((4, 4)),
             dma((2, 4)), dma((2, 4)),
             dma((4,)), dma((4,)),
             dma, dma,
-            dma((2, 8)), dma((2, 8)), dma((2, 7)), dma((2, 7)),
+            dma((2, 2, 8)), dma((2, 2, 8)), dma((2, 2, 7)), dma((2, 2, 7)),
             dma((16,)), dma((8, 2)),
             dma((16,)), dma((16,)),
-            dma((4,)), dma((4,)), dma((4,)), dma((4,)),
+            dma((4, 4)), dma((4, 4)), dma((4, 4)), dma((4, 4)),
             dma((8,)), dma((8,)),
             dma((16,)), dma((16,)),
             dma((16,)), dma((4, 4)),
         ],
         compiler_params=pltpu.CompilerParams(
-            collective_id=0, has_side_effects=True, vmem_limit_bytes=40 * 1024 * 1024
+            collective_id=0, has_side_effects=True, vmem_limit_bytes=63 * 1024 * 1024 + 900 * 1024
         ),
         name="shampoo",
     )(

time: 119 us -> 107 us (0.90)
  Pallas kernels: 109 us -> 103 us
  local copies, waits for them, and re-layouts: 8.27 us -> 2.98 us
    pallas_call x1, Pallas kernels: 109 us -> 103 us  [on_device(): pl.pallas_call(kernel, out_shape=(jax.ShapeDtypeStruct((1, 64, BLK), F32)...]
    unnamed x17 -> x7, local copies, waits for them, and re-layouts: 8.27 us -> 2.98 us
where the time goes in v2:
time: 107 us; the launch traced here: 106 us
  Pallas kernels  103 us (96%)
  local copies, waits for them, and re-layouts  2.98 us (3%)
    pallas_call x1, Pallas kernels, on_device(): pl.pallas_call(kernel, out_shape=(jax.ShapeDtypeStruct((1, 64, BLK), F32)...  103 us
    unnamed x7, local copies, waits for them, and re-layouts  2.98 us

profile of v2, /device:TPU:1, one launch (start us, length us, event | category | flops | bytes accessed | tf_op | source)
XLA Modules:
  0.0 106.4 jit_solution(15785953282672022045)
XLA Ops:
  0.6 102.8 %shampoo.1 = (f32[1,64,512]{2,1,0:T(8,128)}, f32[1,64,512]{2,1,0:T(8,128)}, bf16[16,1024]{1,0:T(8,128)(2,1)}) custom-call(bf16[4,2,32,1024]{3,2,1,0:T(8,128)(2,1)} %bitcast.2, bf16[256,1024]{1,0:T(8,128)(2,1)} %g_ref.1, f32[1,64,512]{2,1,0:T(8,128)} %ls_ref.1, f32[1,64,512]{2,1,0:T(8,128)} %rs_ref.1, f32[1,64,512]{2,1,0:T(8,128)} %lr_ref.1, ...), custom_call_target="tpu_custom_call" | custom-call | tf_op jit(solution)/shard_map/shampoo/pallas_call | solution.py:428
  103.4 0.0 copy-start
  103.4 1.6 %copy.13 = f32[1,64,512]{2,1,0:T(8,128)} copy(f32[1,64,512]{2,1,0:T(8,128)} %get-tuple-element.6) | data formatting | bytes 262144
  105.0 0.0 copy-done
  105.0 0.0 copy-start.1
  105.0 0.7 copy.14
  105.7 0.1 copy-done.1
  105.8 0.6 copy.15
Async XLA Ops:
  103.4 1.6 %copy-start = (f32[1,64,512]{2,1,0:T(8,128)S(1)}, f32[1,64,512]{2,1,0:T(8,128)}, u32[]{:S(2)}) copy-start(f32[1,64,512]{2,1,0:T(8,128)} %get-tuple-element.7) | copy-start | bytes 393220
  105.0 0.8 copy-start.1

commit v3 on v2

--- a/solution.py
+++ b/solution.py
@@ -48,10 +48,10 @@
 def kernel(
     x_ref, g_ref, ls_ref, rs_ref, lr_ref, rr_ref, ob_ref,
     ln_ref, rn_ref, dir_ref,
-    xown, xb1, xb2, xb3, gown, gb1, gb2, gb3, part, ring_m, ring_p, own, r1, sb, hrel, lh, rrb, hhi, hlo, lsv, rsv, lgram,
+    xown, xb1, xb2, xb3, gown, gb1, gb2, gb3, part, ring_1, ring_2, ring_a, own, r1, sb, hrel, lh, rrb, hhi, hlo, lsv, rsv, lgram,
     sq, sq_own, upd, fbuf, sb2, gr, zsel, xsel,
     loc, xs, xr, ys, yr, ds_, dr, gs, gr_s, lsd, lrv, rrs, rrr,
-    rms, rmr, rps, rpr, a_s, a_r, b_s, b_r, c_s, c_r, cd_s, cd_r, e_s, e_r, f_s, f_r, h_s, h_r,
+    r1s, r1r, r2s, r2r, a_s, a_r, b_s, b_r, c_s, c_r, cd_s, cd_r, e_s, e_r, f_s, f_r, h_s, h_r,
 ):
     d = lax.axis_index("dp")
     t = lax.axis_index("tensor")
@@ -80,7 +80,7 @@
 
     barrier = pltpu.get_barrier_semaphore()
     met = [((x + i) % NX, z, t) for i in (1, 3, 2)] + [(x, z, (t + k) % NT) for k in range(1, NT)]
-    met += [(x, (z + k) % NZ, t) for k in (1, NZ - 1)]
+    met += [(x, (z + k) % NZ, t) for k in (1, NZ - 1, 2, NZ - 2)]
     for to_x, to_z, to_t in met:
         pl.semaphore_signal(barrier, inc=1, device_id=(to_x * NZ + to_z, to_t), device_id_type=MESH)
     pl.semaphore_wait(barrier, len(met))
@@ -150,20 +150,43 @@
         for cb, rb, value in gram(act, gb[i]):
             part[cb, rb] += value
 
-    up, down = (z + 1) % NZ, (z + NZ - 1) % NZ
-
     chunks = [(cb, rb) for cb in range(2) for rb in range(2)]
-
-    def minus(q, s, src):
-        return rc(src, ring_m.at[*q, s], rms.at[*q, s], rmr.at[*q, s], x, down, t)
-
-    def plus(q, s, src):
-        return rc(src, ring_p.at[*q, s], rps.at[*q, s], rpr.at[*q, s], x, up, t)
+    ways = (-1, 1)
+
+    def ring_to(way, far):
+        return (z + NZ + way * far) % NZ
+
+    def one(q, way, m, src=None):
+        w = (way + 1) // 2
+        src = part.at[*q, 0] if src is None else src
+        k = m // 2
+        return rc(src, ring_1.at[w, *q, k], r1s.at[w, *q, k], r1r.at[w, *q, k], x, ring_to(way, 1), t)
+
+    def two(q, way, m, src=None):
+        w = (way + 1) // 2
+        src = part.at[*q, 0] if src is None else src
+        k = m // 2 - 1
+        return rc(src, ring_2.at[w, *q, k], r2s.at[w, *q, k], r2r.at[w, *q, k], x, ring_to(way, 2), t)
+
+    def ring_one(m):
+        for q in chunks:
+            for way in ways:
+                one(q, way, m, part.at[*q, ring_to(way, m)]).start()
+
+    def gathered(q, way, m):
+        w = (way + 1) // 2
+        one(q, way, m + 1).wait_recv()
+        total = ring_1[w, *q, m // 2]
+        if m < (8 if way < 0 else 6) - 1:
+            two(q, way, m + 2).wait_recv()
+            total = total + ring_2[w, *q, m // 2]
+        return total
 
     for q in chunks:
-        minus(q, 0, part.at[*q, (z + 8) % NZ]).start()
-        plus(q, 0, part.at[*q, (z + 7) % NZ]).start()
-
+        two(q, -1, 8, part.at[*q, ring_to(-1, 8)]).start()
+        for way in (1, -1):
+            one(q, way, 7, part.at[*q, ring_to(way, 7)]).start()
+    ring_one(5)
     rr_send = rc(rr_ref.at[0], rrb.at[c], rrs, rrr, x, z, sib)
     rr_send.start()
     l_core = y // 2
@@ -178,19 +201,16 @@
     for j in range(1, NY):
         l_send(j).start()
 
-    for s in range(1, 8):
+    for m in (6, 4, 2):
         for q in chunks:
-            minus(q, s - 1, part.at[*q, 0]).wait_recv()
-            ring_m[*q, s - 1] = ring_m[*q, s - 1] + part[*q, (z + 8 + s) % NZ]
-            minus(q, s, ring_m.at[*q, s - 1]).start()
-            if s < 7:
-                plus(q, s - 1, part.at[*q, 0]).wait_recv()
-                ring_p[*q, s - 1] = ring_p[*q, s - 1] + part[*q, (z + 7 - s) % NZ]
-                plus(q, s, ring_p.at[*q, s - 1]).start()
+            for way in ways:
+                w = (way + 1) // 2
+                ring_a[w, *q, m // 2 - 1] = part[*q, ring_to(way, m)] + gathered(q, way, m)
+                two(q, way, m, ring_a.at[w, *q, m // 2 - 1]).start()
+        if m > 2:
+            ring_one(m - 3)
     for q in chunks:
-        plus(q, 6, part.at[*q, 0]).wait_recv()
-        minus(q, 7, part.at[*q, 0]).wait_recv()
-        total = part[*q, z] + (ring_p[*q, 6] + ring_m[*q, 7])
+        total = part[*q, z] + (gathered(q, -1, 0) + gathered(q, 1, 0))
         for row in range(NY):
             own[row, q[1], q[0]] = total[:, row * 128 : row * 128 + 128]
 
@@ -228,7 +248,7 @@
     offset_of = sorted(range(NZ), key=slot_of)
 
     def b_fill(k):
-        block = ob_ref[x * NZ + k]
+        block = ob_ref[x * NZ + (z + k) % NZ]
         safe = jnp.minimum(block, NB - 1)
         for half in range(2):
             value = r1[safe // 4, half, (safe // 2) % 2, safe % 2]
@@ -236,13 +256,15 @@
 
     def b_copy(k):
         to = (z + k) % NZ
-        return rc(sb.at[to], hrel.at[0, 0, slot_of(NZ - k)], b_s.at[k], b_r.at[NZ - k], x, to, t)
-
-    loop(0, NZ, b_fill)
-    b_local = pltpu.make_async_copy(sb.at[z], hrel.at[0, 0, 0], loc.at[9])
-    b_local.start()
-    for o in offset_of[:0:-1]:
-        b_copy(NZ - o).start()
+        return rc(sb.at[k], hrel.at[0, 0, slot_of(NZ - k)], b_s.at[k], b_r.at[NZ - k], x, to, t)
+
+    b_local = pltpu.make_async_copy(sb.at[0], hrel.at[0, 0, 0], loc.at[9])
+    for o in offset_of:
+        b_fill(o)
+        if o == 0:
+            b_local.start()
+        else:
+            b_copy(o).start()
 
     def c_copy(g, j):
         src, dst = hrel.at[0, 0, pl.ds(4 * g, 4)], hrel.at[0, NY - j, pl.ds(4 * g, 4)]
@@ -335,7 +357,8 @@
         to = (z + k) % NZ
         return rc(upd.at[to], fbuf.at[z], f_s.at[k], f_r.at[z], x, to, t)
 
-    loop(1, NZ, lambda k: f_send(k).start())
+    for k in offset_of[:0:-1]:
+        f_send(k).start()
     f_local = pltpu.make_async_copy(upd.at[z], fbuf.at[z], loc.at[10])
     f_local.start()
 
@@ -406,11 +429,12 @@
     for j in range(1, NY):
         l_send(j).wait_send()
 
-    for s in range(8):
-        for q in chunks:
-            minus(q, s, part.at[*q, 0]).wait_send()
-            if s < 7:
-                plus(q, s, part.at[*q, 0]).wait_send()
+    for q in chunks:
+        for way in ways:
+            for m in (7, 5, 3, 1):
+                one(q, way, m).wait_send()
+            for m in (8, 6, 4, 2)[way > 0 :]:
+                two(q, way, m).wait_send()
     pl.when(jnp.logical_not(a_self))(lambda: a_send(0).wait_send())
     loop(1, 16, lambda k: a_send(k).wait_send())
     for k in range(1, NZ):
@@ -444,8 +468,9 @@
             pltpu.VMEM((2, 256, 128), BF16),
             pltpu.VMEM((2, 256, 128), BF16),
             pltpu.VMEM((2, 2, NZ, 8, BLK), F32),
-            pltpu.VMEM((2, 2, 8, 8, BLK), F32),
-            pltpu.VMEM((2, 2, 7, 8, BLK), F32),
+            pltpu.VMEM((2, 2, 2, 4, 8, BLK), F32),
+            pltpu.VMEM((2, 2, 2, 4, 8, BLK), F32),
+            pltpu.VMEM((2, 2, 2, 3, 8, BLK), F32),
             pltpu.VMEM((NY, 2, 2, 8, 128), F32),
             pltpu.VMEM((NT, 2, 2, 2, 8, 128), F32),
             pltpu.VMEM((NZ, 2, 8, 128), F32),
@@ -472,7 +497,7 @@
             dma((2, 4)), dma((2, 4)),
             dma((4,)), dma((4,)),
             dma, dma,
-            dma((2, 2, 8)), dma((2, 2, 8)), dma((2, 2, 7)), dma((2, 2, 7)),
+            dma((2, 2, 2, 4)), dma((2, 2, 2, 4)), dma((2, 2, 2, 4)), dma((2, 2, 2, 4)),
             dma((16,)), dma((8, 2)),
             dma((16,)), dma((16,)),
             dma((4, 4)), dma((4, 4)), dma((4, 4)), dma((4, 4)),

time: 107 us -> 99.5 us (0.930)
  Pallas kernels: 103 us -> 95.7 us
    pallas_call x1, Pallas kernels: 103 us -> 95.7 us  [on_device(): pl.pallas_call(kernel, out_shape=(jax.ShapeDtypeStruct((1, 64, BLK), F32)...]
where the time goes in v3:
time: 99.5 us; the launch traced here: 99.3 us
  Pallas kernels  95.7 us (96%)
  local copies, waits for them, and re-layouts  2.98 us (3%)
    pallas_call x1, Pallas kernels, on_device(): pl.pallas_call(kernel, out_shape=(jax.ShapeDtypeStruct((1, 64, BLK), F32)...  95.7 us
    unnamed x7, local copies, waits for them, and re-layouts  2.98 us

profile of v3, /device:TPU:1, one launch (start us, length us, event | category | flops | bytes accessed | tf_op | source)
XLA Modules:
  0.0 99.3 jit_solution(8021450086287717059)
XLA Ops:
  0.6 95.7 %shampoo.1 = (f32[1,64,512]{2,1,0:T(8,128)}, f32[1,64,512]{2,1,0:T(8,128)}, bf16[16,1024]{1,0:T(8,128)(2,1)}) custom-call(bf16[4,2,32,1024]{3,2,1,0:T(8,128)(2,1)} %bitcast.2, bf16[256,1024]{1,0:T(8,128)(2,1)} %g_ref.1, f32[1,64,512]{2,1,0:T(8,128)} %ls_ref.1, f32[1,64,512]{2,1,0:T(8,128)} %rs_ref.1, f32[1,64,512]{2,1,0:T(8,128)} %lr_ref.1, ...), custom_call_target="tpu_custom_call" | custom-call | tf_op jit(solution)/shard_map/shampoo/pallas_call | solution.py:452
  96.3 0.0 copy-start
  96.4 1.6 %copy.13 = f32[1,64,512]{2,1,0:T(8,128)} copy(f32[1,64,512]{2,1,0:T(8,128)} %get-tuple-element.6) | data formatting | bytes 262144
  98.0 0.0 copy-done
  98.0 0.0 copy-start.1
  98.0 0.7 copy.14
  98.6 0.1 copy-done.1
  98.7 0.6 copy.15
Async XLA Ops:
  96.3 1.6 %copy-start = (f32[1,64,512]{2,1,0:T(8,128)S(1)}, f32[1,64,512]{2,1,0:T(8,128)}, u32[]{:S(2)}) copy-start(f32[1,64,512]{2,1,0:T(8,128)} %get-tuple-element.7) | copy-start | bytes 393220
  98.0 0.8 copy-start.1

commit v4 on v3

--- a/solution.py
+++ b/solution.py
@@ -98,7 +98,7 @@
         columns = pl.ds(pl.multiple_of(cb * BLK + to * 128, 128), 128)
         return rc(g_ref.at[:, columns], gb[NX - i].at[cb], gs.at[cb, i], gr_s.at[cb, NX - i], to, z, t)
 
-    x_send = [x_copy(i, j) for j in (0, 2) for i in order]
+    x_send = [x_copy(i, 0) for i in order] + [x_copy(i, 2) for i in (1, 3)]
     g_send = [g_copy(cb, i) for cb in range(2) for i in order]
     for copy in x_send + g_send:
         copy.start()
@@ -125,7 +125,7 @@
     y_send, d_send = [], []
     for i in order:
         x_copy(NX - i, 0).wait_recv()
-        for j in (1, 3):
+        for j in (1, 3, 2) if i == 2 else (1, 3):
             y_send.append(y_copy(i, j))
             y_send[-1].start()
         d_send.append(core_copy(i, 0))
@@ -133,7 +133,7 @@
 
     for i in order:
         for j in (2, 1, 3):
-            if j == 2:
+            if j == 2 and i != 2:
                 x_copy(NX - i, 2).wait_recv()
             else:
                 y_copy(i, NY - j).wait_recv()
@@ -228,7 +228,8 @@
     a_self = a_core == c
     pl.when(a_self)(lambda: a_local.start())
     pl.when(jnp.logical_not(a_self))(lambda: a_send(0).start())
-    loop(1, 16, lambda k: a_send(k).start())
+    for k in sorted(range(1, 16), key=lambda k: -min(k // 4, 4 - k // 4) - min(k % 4, 4 - k % 4)):
+        a_send(k).start()
     pl.when(a_self)(lambda: a_local.wait())
 
     def a_wait(k):
@@ -368,20 +369,22 @@
     lgram[...] = left.reshape(2, 64, BLK)
     ln_ref[0] = FACTOR_DECAY * lsv[...] + fraction * lgram[c]
 
+    held = [ob_ref[x * NZ + k] for k in range(NZ)]
+
     def find_z(b):
-        def step(k, found):
-            return jnp.where(ob_ref[x * NZ + k] == b, k, found)
-
-        zsel[b] = lax.fori_loop(0, NZ, step, 0)
+        found = 0
+        for k in range(NZ):
+            found = jnp.where(held[k] == b, k, found)
+        zsel[b] = found
 
     loop(0, NB, find_z)
-    for cb in range(2):
-        wanted = t * 4 + (x // 2) * 2 + cb
-
-        def step(k, found):
-            return jnp.where(ob_ref[k] == wanted, k // NZ, found)
-
-        xsel[cb] = lax.fori_loop(0, NX * NZ, step, 0)
+    wanted = t * 4 + (x // 2) * 2
+
+    def find_x(k, found):
+        block = ob_ref[k]
+        return tuple(jnp.where(block == wanted + cb, k // NZ, found[cb]) for cb in range(2))
+
+    xsel[0], xsel[1] = lax.fori_loop(0, NX * NZ, find_x, (0, 0))
 
     def f_wait(k):
         src = (z + k) % NZ

time: 99.5 us -> 95.4 us (0.959)
  Pallas kernels: 95.7 us -> 91.5 us
    pallas_call x1, Pallas kernels: 95.7 us -> 91.5 us  [on_device(): pl.pallas_call(kernel, out_shape=(jax.ShapeDtypeStruct((1, 64, BLK), F32)...]
where the time goes in v4:
time: 95.4 us; the launch traced here: 95.1 us
  Pallas kernels  91.5 us (96%)
  local copies, waits for them, and re-layouts  2.98 us (3%)
    pallas_call x1, Pallas kernels, on_device(): pl.pallas_call(kernel, out_shape=(jax.ShapeDtypeStruct((1, 64, BLK), F32)...  91.5 us
    unnamed x7, local copies, waits for them, and re-layouts  2.98 us

profile of v4, /device:TPU:1, one launch (start us, length us, event | category | flops | bytes accessed | tf_op | source)
XLA Modules:
  0.0 95.1 jit_solution(16077888427514857611)
XLA Ops:
  0.6 91.5 %shampoo.1 = (f32[1,64,512]{2,1,0:T(8,128)}, f32[1,64,512]{2,1,0:T(8,128)}, bf16[16,1024]{1,0:T(8,128)(2,1)}) custom-call(bf16[4,2,32,1024]{3,2,1,0:T(8,128)(2,1)} %bitcast.2, bf16[256,1024]{1,0:T(8,128)(2,1)} %g_ref.1, f32[1,64,512]{2,1,0:T(8,128)} %ls_ref.1, f32[1,64,512]{2,1,0:T(8,128)} %rs_ref.1, f32[1,64,512]{2,1,0:T(8,128)} %lr_ref.1, ...), custom_call_target="tpu_custom_call" | custom-call | tf_op jit(solution)/shard_map/shampoo/pallas_call | solution.py:455
  92.2 0.0 copy-start
  92.2 1.6 %copy.13 = f32[1,64,512]{2,1,0:T(8,128)} copy(f32[1,64,512]{2,1,0:T(8,128)} %get-tuple-element.6) | data formatting | bytes 262144
  93.8 0.0 copy-done
  93.8 0.0 copy-start.1
  93.8 0.7 copy.14
  94.4 0.1 copy-done.1
  94.5 0.6 copy.15
Async XLA Ops:
  92.2 1.6 %copy-start = (f32[1,64,512]{2,1,0:T(8,128)S(1)}, f32[1,64,512]{2,1,0:T(8,128)}, u32[]{:S(2)}) copy-start(f32[1,64,512]{2,1,0:T(8,128)} %get-tuple-element.7) | copy-start | bytes 393220
  93.8 0.8 copy-start.1

commit v5 on v4

--- a/solution.py
+++ b/solution.py
@@ -230,6 +230,8 @@
     pl.when(jnp.logical_not(a_self))(lambda: a_send(0).start())
     for k in sorted(range(1, 16), key=lambda k: -min(k // 4, 4 - k // 4) - min(k % 4, 4 - k % 4)):
         a_send(k).start()
+    for copy in x_send + g_send + y_send + d_send:
+        copy.wait_send()
     pl.when(a_self)(lambda: a_local.wait())
 
     def a_wait(k):
@@ -346,7 +348,9 @@
     rows = pl.ds(pl.multiple_of(t * 64, 64), 64)
     local[5].wait()
     right = dot3((hhi[rows, :], hlo[rows, :]), h2, NTR)
-    rn_ref[0] = FACTOR_DECAY * rsv[...] + fraction * right
+    rsv[...] = FACTOR_DECAY * rsv[...] + fraction * right
+    r_out = pltpu.make_async_copy(rsv, rn_ref.at[0], loc.at[11])
+    r_out.start()
 
     for k in range(1, NT):
         e_copy(k).wait_recv()
@@ -367,7 +371,9 @@
     lanes = pl.ds(pl.multiple_of(y * 128, 128), 128)
     left = dot3((hhi[:, lanes], hlo[:, lanes]), h2, TN)
     lgram[...] = left.reshape(2, 64, BLK)
-    ln_ref[0] = FACTOR_DECAY * lsv[...] + fraction * lgram[c]
+    lsv[...] = FACTOR_DECAY * lsv[...] + fraction * lgram[c]
+    l_out = pltpu.make_async_copy(lsv, ln_ref.at[0], loc.at[12])
+    l_out.start()
 
     held = [ob_ref[x * NZ + k] for k in range(NZ)]
 
@@ -386,47 +392,7 @@
 
     xsel[0], xsel[1] = lax.fori_loop(0, NX * NZ, find_x, (0, 0))
 
-    def f_wait(k):
-        src = (z + k) % NZ
-        rc(fbuf.at[src], fbuf.at[src], f_s.at[k], f_r.at[src], x, src, t).wait_recv()
-
-    loop(1, NZ, f_wait)
-    f_local.wait()
-
-    def h_fill(k):
-        rb, to_t = k // NT, k % NT
-        for cb in range(2):
-            sb2[k, cb] = fbuf[zsel[to_t * 4 + rb * 2 + cb]]
-
-    def h_is_self(k):
-        return jnp.logical_and(c + 2 * (k // NT) == x, k % NT == t)
-
-    def h_send(k):
-        return rc(sb2.at[k], gr.at[x, y], h_s.at[k], h_r.at[x, y], c + 2 * (k // NT), z, k % NT)
-
-    def h_start(k):
-        pl.when(h_is_self(k))(lambda: pltpu.make_async_copy(sb2.at[k], gr.at[x, y], loc.at[8]).start())
-        pl.when(jnp.logical_not(h_is_self(k)))(lambda: h_send(k).start())
-
-    loop(0, 16, h_fill)
-    loop(0, 16, h_start)
-
-    def h_wait(k):
-        from_x, from_y = k // NY, k % NY
-        from_t = from_y * 2 + x % 2
-        same = jnp.logical_and(from_x == x, from_t == t)
-        place = gr.at[from_x, from_y]
-        pl.when(same)(lambda: pltpu.make_async_copy(place, place, loc.at[8]).wait())
-        pl.when(jnp.logical_not(same))(
-            lambda: rc(place, place, h_s.at[0], h_r.at[from_x, from_y], from_x, z, from_t).wait_recv()
-        )
-
-    loop(0, 16, h_wait)
-    for cb in range(2):
-        for row in range(NY):
-            dir_ref[:, cb * BLK + row * 128 : cb * BLK + (row + 1) * 128] = gr[xsel[cb], row, cb]
-
-    for copy in x_send + g_send + y_send + d_send + c_send + cd_send + [rr_send]:
+    for copy in c_send + cd_send + [rr_send]:
         copy.wait_send()
     pl.when(jnp.logical_not(l_self))(lambda: l_send(0).wait_send())
     for j in range(1, NY):
@@ -442,6 +408,50 @@
     loop(1, 16, lambda k: a_send(k).wait_send())
     for k in range(1, NZ):
         b_copy(k).wait_send()
+
+    def f_wait(k):
+        src = (z + k) % NZ
+        rc(fbuf.at[src], fbuf.at[src], f_s.at[k], f_r.at[src], x, src, t).wait_recv()
+
+    loop(1, NZ, f_wait)
+    f_local.wait()
+
+    def h_fill(k):
+        rb, to_t = k // NT, k % NT
+        for cb in range(2):
+            sb2[k, cb] = fbuf[zsel[to_t * 4 + rb * 2 + cb]]
+
+    def h_is_self(k):
+        return jnp.logical_and(c + 2 * (k // NT) == x, k % NT == t)
+
+    def h_send(k):
+        return rc(sb2.at[k], gr.at[x, y], h_s.at[k], h_r.at[x, y], c + 2 * (k // NT), z, k % NT)
+
+    def h_start(k):
+        pl.when(h_is_self(k))(lambda: pltpu.make_async_copy(sb2.at[k], gr.at[x, y], loc.at[8]).start())
+        pl.when(jnp.logical_not(h_is_self(k)))(lambda: h_send(k).start())
+
+    for k in range(16):
+        h_fill(k)
+        h_start(k)
+
+    def h_wait(k):
+        from_x, from_y = k // NY, k % NY
+        from_t = from_y * 2 + x % 2
+        same = jnp.logical_and(from_x == x, from_t == t)
+        place = gr.at[from_x, from_y]
+        pl.when(same)(lambda: pltpu.make_async_copy(place, place, loc.at[8]).wait())
+        pl.when(jnp.logical_not(same))(
+            lambda: rc(place, place, h_s.at[0], h_r.at[from_x, from_y], from_x, z, from_t).wait_recv()
+        )
+
+    loop(0, 16, h_wait)
+    for cb in range(2):
+        for row in range(NY):
+            dir_ref[:, cb * BLK + row * 128 : cb * BLK + (row + 1) * 128] = gr[xsel[cb], row, cb]
+
+    r_out.wait()
+    l_out.wait()
     for k in range(1, NT):
         e_copy(k).wait_send()
     loop(1, NZ, lambda k: f_send(k).wait_send())
@@ -460,7 +470,7 @@
             jax.ShapeDtypeStruct((16, 1024), BF16),
         ),
         in_specs=[anywhere] * 6 + [pl.BlockSpec(memory_space=pltpu.SMEM)],
-        out_specs=(in_vmem, in_vmem, in_vmem),
+        out_specs=(anywhere, anywhere, in_vmem),
         scratch_shapes=[
             pltpu.VMEM((NY, 2, 32, 1024), BF16),
             pltpu.VMEM((NY, 2, 32, 1024), BF16),
@@ -493,7 +503,7 @@
             pltpu.VMEM((NX, NY, 2, 16, 128), BF16),
             pltpu.SMEM((NB,), jnp.int32),
             pltpu.SMEM((2,), jnp.int32),
-            dma((11,)),
+            dma((13,)),
             dma((4, 4)), dma((4, 4)),
             dma((4, 4)), dma((4, 4)),
             dma((4, 4)), dma((4, 4)),

time: 95.4 us -> 94.8 us (level)
  no operation moved by 1% of the time
where the time goes in v5:
time: 94.8 us; the launch traced here: 94.6 us
  Pallas kernels  91 us (96%)
  local copies, waits for them, and re-layouts  2.98 us (3%)
    pallas_call x1, Pallas kernels, on_device(): pl.pallas_call(kernel, out_shape=(jax.ShapeDtypeStruct((1, 64, BLK), F32)...  91 us
    unnamed x7, local copies, waits for them, and re-layouts  2.98 us

profile of v5, /device:TPU:1, one launch (start us, length us, event | category | flops | bytes accessed | tf_op | source)
XLA Modules:
  0.0 94.6 jit_solution(14432954693320182181)
XLA Ops:
  0.6 91.0 %shampoo.1 = (f32[1,64,512]{2,1,0:T(8,128)}, f32[1,64,512]{2,1,0:T(8,128)}, bf16[16,1024]{1,0:T(8,128)(2,1)}) custom-call(bf16[4,2,32,1024]{3,2,1,0:T(8,128)(2,1)} %bitcast.2, bf16[256,1024]{1,0:T(8,128)(2,1)} %g_ref.1, f32[1,64,512]{2,1,0:T(8,128)} %ls_ref.1, f32[1,64,512]{2,1,0:T(8,128)} %rs_ref.1, f32[1,64,512]{2,1,0:T(8,128)} %lr_ref.1, ...), custom_call_target="tpu_custom_call" | custom-call | tf_op jit(solution)/shard_map/shampoo/pallas_call | solution.py:465
  91.6 0.0 copy-start
  91.6 1.6 %copy.13 = f32[1,64,512]{2,1,0:T(8,128)} copy(f32[1,64,512]{2,1,0:T(8,128)} %get-tuple-element.6) | data formatting | bytes 262144
  93.2 0.0 copy-done
  93.3 0.0 copy-start.1
  93.3 0.7 copy.14
  93.9 0.1 copy-done.1
  94.0 0.6 copy.15
Async XLA Ops:
  91.6 1.6 %copy-start = (f32[1,64,512]{2,1,0:T(8,128)S(1)}, f32[1,64,512]{2,1,0:T(8,128)}, u32[]{:S(2)}) copy-start(f32[1,64,512]{2,1,0:T(8,128)} %get-tuple-element.7) | copy-start | bytes 393220
  93.3 0.8 copy-start.1
